TPU v7x, 256 devices: a whole 4x4x8 slice. The times are simulated.
256 devices in a mesh: blk: 64 (over y, z, x_lo), hid: 4 (over x_hi, core).
Axes of the slice: x: 4 (x_hi: 2, x_lo: 2; x = x_hi * 2 + x_lo), y: 4, z: 8, core: 2. Of those that a mesh axis runs over, the one named last changes fastest.
Arguments:
- gate_pre: bfloat16 [20480, 7168], P('blk', 'hid'), may hold values from -8 to 8
- up_pre: bfloat16 [20480, 7168], P('blk', 'hid'), may hold values from -6 to 6
- down_weight: bfloat16 [2560, 7168], P('blk', 'hid'), may hold values from -0.0625 to 0.0625
- cotangent: bfloat16 [20480, 2560], P('blk', 'hid'), may hold values from -16 to 16
Outputs:
- mixed: bfloat16 [20480, 2560], P('blk', 'hid')
- grad_gate: bfloat16 [20480, 7168], P('blk', 'hid')
- grad_up: bfloat16 [20480, 7168], P('blk', 'hid')
- weight_grad: float32 [2560, 7168], P('blk', 'hid')
All inputs are finite; a program needn't handle non-finite values.
Results may differ from a plain program's by a relative error of at most 0.0049.
Values may be sent and summed in bfloat16 or wider, within the bound.
No kernel may reach another device: no remote copies, remote signals or barrier semaphores. Data moves between devices by JAX's collectives and lax.ppermute only.
A program may use at most 384 MiB of HBM per device.

v0:
```python
import jax
import jax.numpy as jnp
from jax import lax
from jax.sharding import PartitionSpec as P


def shards(gate_pre, up_pre, down_weight, cotangent):
    gate_value = gate_pre.astype(jnp.float32)
    up_value = up_pre.astype(jnp.float32)
    sigmoid_gate = jax.nn.sigmoid(gate_value)
    activated = gate_value * sigmoid_gate
    hidden = (activated * up_value).astype(jnp.bfloat16)
    contract_last = (((1,), (1,)), ((), ()))
    contract_first = (((0,), (0,)), ((), ()))
    full_weight = lax.all_gather(down_weight, "blk", axis=0, tiled=True)
    partial_value = lax.dot_general(
        hidden, full_weight, contract_last, preferred_element_type=jnp.float32
    )
    mixed = lax.psum_scatter(partial_value, "hid", scatter_dimension=1, tiled=True).astype(
        jnp.bfloat16
    )
    cotangent_all = lax.all_gather(cotangent, "hid", axis=1, tiled=True)
    grad_hidden = jnp.dot(cotangent_all, full_weight, preferred_element_type=jnp.float32)
    grad_gate = (
        grad_hidden * up_value * sigmoid_gate * (1.0 + gate_value * (1.0 - sigmoid_gate))
    ).astype(jnp.bfloat16)
    grad_up = (grad_hidden * activated).astype(jnp.bfloat16)
    weight_grad = lax.psum_scatter(
        lax.dot_general(cotangent_all, hidden, contract_first, preferred_element_type=jnp.float32),
        "blk",
        scatter_dimension=0,
        tiled=True,
    )
    return (mixed, grad_gate, grad_up, weight_grad)


def solution(mesh):
    placed = (P("blk", "hid"), P("blk", "hid"), P("blk", "hid"), P("blk", "hid"))
    return jax.shard_map(
        shards,
        mesh=mesh,
        in_specs=placed,
        out_specs=(P("blk", "hid"), P("blk", "hid"), P("blk", "hid"), P("blk", "hid")),
        check_vma=False,
    )
```

profile of v0, /device:TPU:4, one launch (start us, length us, event | category | flops | bytes accessed | tf_op | source)
XLA Modules:
  0.0 820.8 jit_solution(11549528642300104054)
XLA Ops:
  7.2 0.0 all-gather.3.cloned.1.call-start
  7.2 0.7 all-gather.3.cloned.1.call-update
  7.9 0.0 all-gather.5.cloned.1.call-start
  7.9 0.7 all-gather.5.cloned.1.call-update
  8.6 0.0 reduce-scatter.5.cloned.1.call-start
  8.7 320.9 %all-gather.3.cloned.1.call-done = bf16[2560,1792]{1,0:T(8,128)(2,1)} async-done(((bf16[40,1792]{1,0:T(8,128)(2,1)}), bf16[2560,1792]{1,0:T(8,128)(2,1)}) %all-gather.3.cloned.1.call-update) | async-done | bytes 9175056 | tf_op jit(solution)/shard_map/all_gather | solution.py:15
  329.6 9.3 %fusion.9 = f32[320,2560]{1,0:T(8,128)} fusion(bf16[2560,1792]{1,0:T(8,128)(2,1)} %all-gather.3.cloned.1.call-done, bf16[320,1792]{1,0:T(8,128)(2,1)} %param.5, bf16[320,1792]{1,0:T(8,128)(2,1)} %param.4), kind=kOutput, calls=%fused_computation.15 | convolution fusion | flops 2940600320 | bytes 14745600 | tf_op jit(solution)/shard_map/dot_general | solution.py:16
  338.8 0.0 copy-start
  338.8 0.0 copy-start.1
  338.8 0.0 reduce-scatter.5.cloned.1.call-update
  338.9 0.0 reduce-scatter.7.cloned.1.call-start
  338.9 12.7 %all-gather.5.cloned.1.call-done = bf16[320,2560]{1,0:T(8,128)(2,1)} async-done(((bf16[320,640]{1,0:T(8,128)(2,1)}), bf16[320,2560]{1,0:T(8,128)(2,1)}) %all-gather.5.cloned.1.call-update) | async-done | bytes 1638416 | tf_op jit(solution)/shard_map/all_gather | solution.py:22
  351.6 0.0 copy-done
  351.6 0.0 copy-done.1
  351.6 10.3 %convolution_bitcast_fusion = f32[2560,1792]{0,1:T(8,128)} fusion(bf16[320,2560]{1,0:T(8,128)(2,1)} %all-gather.5.cloned.1.call-done, bf16[320,1792]{1,0:T(8,128)(2,1)S(1)} %copy-done, bf16[320,1792]{1,0:T(8,128)(2,1)S(1)} %copy-done.1), kind=kOutput, calls=%fused_computation | convolution fusion | flops 2940600320 | bytes 22282240 | tf_op jit(solution)/shard_map/dot_general | solution.py:29
  362.0 19.6 %copy.10 = f32[2560,1792]{1,0:T(8,128)} copy(f32[2560,1792]{0,1:T(8,128)} %convolution_bitcast_fusion) | data formatting | bytes 36700160
  381.6 0.0 reduce-scatter.7.cloned.1.call-update
  381.6 9.3 %multiply_convert_fusion = (bf16[320,1792]{1,0:T(8,128)(2,1)}, bf16[320,1792]{1,0:T(8,128)(2,1)}) fusion(bf16[320,1792]{1,0:T(8,128)(2,1)S(1)} %copy-done.1, bf16[320,1792]{1,0:T(8,128)(2,1)S(1)} %copy-done, bf16[320,2560]{1,0:T(8,128)(2,1)} %all-gather.5.cloned.1.call-done, bf16[2560,1792]{1,0:T(8,128)(2,1)} %all-gather.3.cloned.1.call-done), kind=kOutput, calls=%fused_computation.14 | convolution fusion | flops 2944614400 | bytes 15400960 | tf_op jit(solution)/shard_map/dot_general | solution.py:23
  390.9 13.8 %reduce-scatter.5.cloned.1.call-done = f32[320,640]{1,0:T(8,128)} async-done(((f32[320,2560]{1,0:T(8,128)}), f32[320,640]{1,0:T(8,128)}) %reduce-scatter.5.cloned.1.call-update) | async-done | bytes 819216 | tf_op jit(solution)/shard_map/reduce_scatter | solution.py:19
  404.7 1.9 convert_element_type.21
  406.6 407.6 %reduce-scatter.7.cloned.1.call-done = f32[40,1792]{1,0:T(8,128)} async-done(((f32[2560,1792]{1,0:T(8,128)}), f32[40,1792]{1,0:T(8,128)}) %reduce-scatter.7.cloned.1.call-update) | async-done | bytes 286736
Async XLA Ops:
  7.2 322.4 %all-gather.3.cloned.1.call-start = ((), (), s32[]{:S(2)}) async-start(), calls=%async_computation.2 | async-start | bytes 9318400 | tf_op jit(solution)/shard_map/all_gather | solution.py:15
  7.9 343.7 %all-gather.5.cloned.1.call-start = ((), (), s32[]{:S(2)}) async-start(), calls=%async_computation.4 | async-start | bytes 2048000 | tf_op jit(solution)/shard_map/all_gather | solution.py:22
  8.6 396.1 %reduce-scatter.5.cloned.1.call-start = ((), (), s32[]{:S(2)}) async-start(), calls=%async_computation.3 | async-start | bytes 4096000 | tf_op jit(solution)/shard_map/reduce_scatter | solution.py:19
  338.8 12.8 %copy-start = (bf16[320,1792]{1,0:T(8,128)(2,1)S(1)}, bf16[320,1792]{1,0:T(8,128)(2,1)}, u32[]{:S(2)}) copy-start(bf16[320,1792]{1,0:T(8,128)(2,1)} %param.5) | copy-start | bytes 3440644
  338.8 12.8 %copy-start.1 = (bf16[320,1792]{1,0:T(8,128)(2,1)S(1)}, bf16[320,1792]{1,0:T(8,128)(2,1)}, u32[]{:S(2)}) copy-start(bf16[320,1792]{1,0:T(8,128)(2,1)} %param.4) | copy-start | bytes 3440644
  338.9 475.4 %reduce-scatter.7.cloned.1.call-start = ((), (), s32[]{:S(2)}) async-start(), calls=%async_computation.5 | async-start | bytes 18636800
Sparse Core Ops, SparseCore 0:
  9.8 319.7 all-gather.2
  331.4 20.1 all-gather.4
  354.4 50.2 reduce-scatter.4
  407.9 406.3 reduce-scatter.6
where the time goes:
time: 821 us
  waiting for transfers between devices  756 us (92%)
  matrix products  28.9 us (4%)
  local copies, waits for them, and re-layouts  19.6 us (2%)
  between operations  13.8 us (2%)
    unnamed x5, waiting for transfers between devices  409 us
    all_gather x1, waiting for transfers between devices, shards(): full_weight = lax.all_gather(down_weight, 'blk', axis=0, tiled=True)  321 us
    unnamed x5, local copies, waits for them, and re-layouts  19.6 us
  transfers between devices with their start and end apart: 4, of which 4 were waited for; matrix products, arithmetic and copies ran while one was open for 6% of the time, Pallas kernels for 0%

commit v1 on v0

v1 whole, which is shorter than its diff:
```python
import jax
import jax.numpy as jnp
import numpy as np
from jax import lax
from jax.sharding import Mesh, PartitionSpec as P

SIZES = {"y": 4, "z": 8, "xl": 2, "xh": 2, "c": 2}
CUTS = ((0, 896), (896, 1792))


def shift(value, axis, step):
    n = SIZES[axis]
    return lax.ppermute(value, axis, [(i, (i + step) % n) for i in range(n)])


def shift_x(value, step):
    def place(x):
        return (x % 2) * 2 + x // 2

    return lax.ppermute(value, ("xl", "xh"), [(place(x), place((x + step) % 4)) for x in range(4)])


def regroup():
    order = np.arange(640).reshape(8, 2, 40).transpose(1, 0, 2).reshape(-1)
    return np.eye(640, dtype=np.float32)[order].astype(jnp.bfloat16)


def dot(a, b, ca, cb, kind=jnp.float32):
    return lax.dot_general(a, b, (((ca,), (cb,)), ((), ())), preferred_element_type=jnp.float32).astype(kind)


def pick(flag, a, b):
    return jnp.where(flag, a, b)


def shards(gate_pre, up_pre, down_weight, cotangent):
    bf16 = jnp.bfloat16
    iy, iz, ixl, ixh, ic = (lax.axis_index(a) for a in ("y", "z", "xl", "xh", "c"))
    low, first, core0 = ixl == 0, ixh == 0, ic == 0
    gate_value = gate_pre.astype(jnp.float32)
    up_value = up_pre.astype(jnp.float32)
    sigmoid_gate = jax.nn.sigmoid(gate_value)
    activated = gate_value * sigmoid_gate
    hidden = (activated * up_value).astype(bf16)
    order = jnp.asarray(regroup())

    weights = [lax.all_gather(down_weight[:, a:b], ("y", "z"), axis=0, tiled=True) for a, b in CUTS]

    turned = dot(order, cotangent, 1, 1, bf16).reshape(2, 320, 320)
    own_part = lax.dynamic_index_in_dim(turned, ixl, 0, False)
    other_part = lax.dynamic_index_in_dim(turned, 1 - ixl, 0, False)
    from_left = shift_x(other_part, 1)
    from_right = shift_x(other_part, -1)
    from_far = shift_x(own_part, 2)
    mine = jnp.stack([own_part, from_far, pick(low, from_right, from_left), pick(low, from_left, from_right)])
    theirs = shift(mine, "c", 1)

    def whole(same, other):
        here = [pick(core0, mine[same], theirs[same]), pick(core0, theirs[same], mine[same])]
        there = [pick(core0, mine[other], theirs[other]), pick(core0, theirs[other], mine[other])]
        blocks = [pick(first, here[0], there[0]), pick(first, here[1], there[1])]
        blocks += [pick(first, there[0], here[0]), pick(first, there[1], here[1])]
        return jnp.concatenate(blocks, axis=0)

    cot_own, cot_pair = whole(0, 1), whole(2, 3)
    own_hidden = [hidden[:, a:b] for a, b in CUTS]
    pair_hidden = [shift(h, "xl", 1) for h in own_hidden]

    cot_own4, cot_pair4 = cot_own.reshape(4, 8, 40, 320), cot_pair.reshape(4, 8, 40, 320)

    def block(z, q):
        rows = [lax.dynamic_index_in_dim(t, z % 8, 1, False).reshape(160, 320) for t in (cot_own4, cot_pair4)]
        return dot(rows[0], own_hidden[q], 1, 0) + dot(rows[1], pair_hidden[q], 1, 0)

    sums = []
    for q in range(2):
        running = {}
        for way, hops in ((1, 4 - q), (-1, 3 + q)):
            value = block(iz + way * hops, q)
            for left in range(hops - 1, -1, -1):
                got = shift(value.astype(bf16), "z", way)
                value = got.astype(jnp.float32)
                if left:
                    value = value + block(iz + way * left, q)
            running[way] = value
        sums.append((running[1] + running[-1] + block(iz, q)).reshape(4, 40, 896))
    summed = jnp.concatenate(sums, axis=2)
    weight_grad = lax.dynamic_index_in_dim(summed, iy, 0, False)
    for step in (1, 2, 3):
        part = lax.dynamic_index_in_dim(summed, (iy + step) % 4, 0, False).astype(bf16)
        weight_grad = weight_grad + shift(part, "y", step).astype(jnp.float32)

    grads = []
    for q in range(2):
        sent = shift(dot(cot_pair, weights[q], 0, 0, bf16), "xl", 1)
        grads.append(dot(cot_own, weights[q], 0, 0) + sent.astype(jnp.float32))
    grad_hidden = jnp.concatenate(grads, axis=1)
    grad_gate = (
        grad_hidden * up_value * sigmoid_gate * (1.0 + gate_value * (1.0 - sigmoid_gate))
    ).astype(bf16)
    grad_up = (grad_hidden * activated).astype(bf16)

    def partial(h):
        return sum(dot(weights[q], h[q], 1, 1) for q in range(2)).reshape(2, 2, 320, 320)

    out_own, out_pair = partial(own_hidden), partial(pair_hidden)
    both = jnp.stack([out_own, out_pair])
    keep = lax.dynamic_index_in_dim(both, ic, 2, False)
    give = lax.dynamic_index_in_dim(both, 1 - ic, 2, False).astype(bf16)
    added = keep + shift(give, "c", 1).astype(jnp.float32)
    near = lax.dynamic_index_in_dim(added, ixh, 1, False)
    far = lax.dynamic_index_in_dim(added, 1 - ixh, 1, False).astype(bf16)
    near_pair = near[1].astype(bf16)
    left = shift_x(pick(low, near_pair, far[1]), 1)
    right = shift_x(pick(low, far[1], near_pair), -1)
    across = shift_x(far[0], 2)
    own_rows = (near[0] + across.astype(jnp.float32)).astype(bf16)
    other_rows = (left.astype(jnp.float32) + right.astype(jnp.float32)).astype(bf16)
    rows = jnp.concatenate([pick(low, own_rows, other_rows), pick(low, other_rows, own_rows)], axis=0)
    mixed = dot(rows, order, 0, 0, bf16)
    return (mixed, grad_gate, grad_up, weight_grad)


def solution(mesh):
    fine = Mesh(mesh.devices.reshape(4, 8, 2, 2, 2), ("y", "z", "xl", "xh", "c"))
    placed = P(("y", "z", "xl"), ("xh", "c"))
    return jax.shard_map(
        shards,
        mesh=fine,
        in_specs=(placed,) * 4,
        out_specs=(placed,) * 4,
        check_vma=False,
    )
```

time: 821 us -> 320 us (0.39)
  waiting for transfers between devices: 756 us -> 181 us
  starting transfers between devices: 0.16 us -> 37.5 us
  matrix products: 28.9 us -> 51.6 us
    unnamed x5 -> x2, waiting for transfers between devices: 409 us -> 0.71 us
    all_gather x2, waiting for transfers between devices: 334 us -> 135 us  [shards(): lax.all_gather(down_weight[:, a:b], ('y', 'z'), axis=0, tiled=True)]
    ppermute x0 -> x29, waiting for transfers between devices: none -> 45.6 us  [the longest x23 29.2 us: shift(): return lax.ppermute(value, axis, [(i, (i + step) % n) for i in range(n)])]
    ppermute x0 -> x29, starting transfers between devices: none -> 37.4 us  [the longest x23 30.7 us: shift(): return lax.ppermute(value, axis, [(i, (i + step) % n) for i in range(n)])]
    dot_general x3 -> x43, matrix products: 28.9 us -> 51.6 us  [dot(): lax.dot_general(a, b, (((ca,), (cb,)), ((), ())), preferred_element_type=...]
    unnamed x5 -> x82, local copies, waits for them, and re-layouts: 19.6 us -> 2.13 us
    another operation x0 -> x4, local copies, waits for them, and re-layouts: none -> 15.5 us  [shards(): both = jnp.stack([out_own, out_pair])]
    reduce_scatter x1 -> x0, waiting for transfers between devices: 13.8 us -> none  [shards(): lax.psum_scatter(partial_value, 'hid', scatter_dimension=1, tiled=True)]
  transfers between devices with their start and end apart: 4 -> 31, of which waited for: 4 -> 21; matrix products, arithmetic and copies ran while one was open for 6% -> 17% of each run, Pallas kernels for 0% -> 0%
where the time goes in v1:
time: 320 us; the launch traced here: 314 us
  waiting for transfers between devices  181 us (57%)
  matrix products  51.6 us (16%)
  starting transfers between devices  37.5 us (12%)
  local copies, waits for them, and re-layouts  21.8 us (7%)
  between operations  15.4 us (5%)
  other arithmetic  6.11 us (2%)
    all_gather x2, waiting for transfers between devices, shards(): lax.all_gather(down_weight[:, a:b], ('y', 'z'), axis=0, tiled=True)  135 us
    dot_general x43, matrix products, dot(): lax.dot_general(a, b, (((ca,), (cb,)), ((), ())), preferred_element_type=...  51.6 us
    ppermute x23, starting transfers between devices, shift(): return lax.ppermute(value, axis, [(i, (i + step) % n) for i in range(n)])  30.7 us
    ppermute x23, waiting for transfers between devices, shift(): return lax.ppermute(value, axis, [(i, (i + step) % n) for i in range(n)])  29.2 us
    ppermute x6, waiting for transfers between devices, shift_x(): lax.ppermute(value, ('xl', 'xh'), [(place(x), place((x + step) % 4)) for...  16.4 us
    another operation x4, local copies, waits for them, and re-layouts, shards(): both = jnp.stack([out_own, out_pair])  15.5 us
    ppermute x6, starting transfers between devices, shift_x(): lax.ppermute(value, ('xl', 'xh'), [(place(x), place((x + step) % 4)) for...  6.74 us
  transfers between devices with their start and end apart: 31, of which 21 were waited for; matrix products, arithmetic and copies ran while one was open for 17% of the time, Pallas kernels for 0%

profile of v1, /device:TPU:4, one launch (start us, length us, event | category | flops | bytes accessed | tf_op | source)
XLA Modules:
  0.0 313.7 jit_solution(1204211274499774081)
XLA Ops:
  7.2 1.6 fusion.78
  9.7 1.7 convolution_convert_fusion.2
  12.3 1.5 collective-permute-start.8
  13.8 2.2 collective-permute-start.6
  16.0 4.6 %collective-permute-done.7 = bf16[320,320]{1,0:T(8,128)(2,1)S(1)} collective-permute-done((bf16[320,320]{1,0:T(8,128)(2,1)S(1)}, bf16[320,320]{1,0:T(8,128)(2,1)S(1)}, u32[]{:S(2)}, u32[]{:S(2)}) %collective-permute-start.7) | collective-permute-done | bytes 204832 | tf_op jit(solution)/shard_map/ppermute | solution.py:20
  21.0 5.0 %collective-permute-done.6 = bf16[320,320]{1,0:T(8,128)(2,1)S(1)} collective-permute-done((bf16[320,320]{1,0:T(8,128)(2,1)S(1)}, bf16[320,320]{1,0:T(8,128)(2,1)S(1)}, u32[]{:S(2)}, u32[]{:S(2)}) %collective-permute-start.6) | collective-permute-done | bytes 204832 | tf_op jit(solution)/shard_map/ppermute | solution.py:20
  26.5 2.4 collective-permute-done.9
  30.5 61.8 %all-gather.3.cloned.1.call-done = bf16[1280,896]{1,0:T(8,128)(2,1)} async-done(((bf16[40,896]{1,0:T(8,128)(2,1)}), bf16[1280,896]{1,0:T(8,128)(2,1)}) %all-gather.3.cloned.1.call-update) | async-done | bytes 2293776 | tf_op jit(solution)/shard_map/all_gather | solution.py:47
  92.2 4.0 %convolution_convert_fusion.1 = bf16[320,896]{1,0:T(8,128)(2,1)} fusion(bf16[1280,896]{1,0:T(8,128)(2,1)} %all-gather.3.cloned.1.call-done, bf16[320,320]{1,0:T(8,128)(2,1)} %copy-done.36, bf16[320,320]{1,0:T(8,128)(2,1)} %copy-done.34, bf16[320,320]{1,0:T(8,128)(2,1)} %copy-done.32, bf16[320,320]{1,0:T(8,128)(2,1)} %copy-done.30), kind=kOutput, calls=%fused_computation.39 | convolution fusion | flops 737566720 | bytes 3686400 | tf_op jit(solution)/shard_map/dot_general | solution.py:29
  96.2 1.2 collective-permute-start.10
  97.4 73.2 %all-gather.5.cloned.1.call-done = bf16[1280,896]{1,0:T(8,128)(2,1)} async-done(((bf16[40,896]{1,0:T(8,128)(2,1)}), bf16[1280,896]{1,0:T(8,128)(2,1)}) %all-gather.5.cloned.1.call-update) | async-done | bytes 2293776 | tf_op jit(solution)/shard_map/all_gather | solution.py:47
  170.6 2.7 convolution_convert_fusion
  173.3 1.4 collective-permute-start.11
  176.8 2.1 convolution_add_fusion.3
  178.9 5.4 %collective-permute-done.11 = bf16[320,896]{1,0:T(8,128)(2,1)S(1)} collective-permute-done((bf16[320,896]{1,0:T(8,128)(2,1)S(1)}, bf16[320,896]{1,0:T(8,128)(2,1)S(1)}, u32[]{:S(2)}, u32[]{:S(2)}) %collective-permute-start.11) | collective-permute-done | bytes 573472 | tf_op jit(solution)/shard_map/ppermute | solution.py:13
  185.4 2.7 multiply_convert_fusion
  188.1 1.1 fusion.77
  189.2 1.2 fusion.42
  190.3 1.2 fusion.59
  191.5 1.2 fusion.52
  192.7 1.2 fusion.67
  193.9 1.1 fusion.54
  195.0 1.2 fusion.69
  196.1 1.1 fusion.56
  197.3 1.2 fusion.71
  198.5 1.1 fusion.44
  199.6 1.1 fusion.61
  200.7 1.1 fusion.46
  201.9 1.2 fusion.63
  203.1 1.1 fusion.48
  204.2 1.2 fusion.65
  205.3 1.2 collective-permute-start.1
  209.5 1.1 fusion.50
  210.6 1.1 fusion.73
  211.8 2.8 stack_reshape.6
  214.6 3.9 %copy.15 = f32[1,2,2,320,320]{4,3,1,0,2:T(8,128)S(1)} copy(f32[1,2,2,320,320]{3,2,1,4,0:T(2,128)} %stack_reshape.6) | data formatting | bytes 3276800 | tf_op jit(solution)/shard_map/stack;reshape | solution.py:107
  218.5 2.9 collective-permute-done.1
  221.5 2.2 fusion.18
  224.8 2.3 fusion.19
  227.1 2.4 collective-permute-start.22
  231.6 3.2 %collective-permute-start.16 = (bf16[160,896]{1,0:T(8,128)(2,1)}, bf16[160,896]{1,0:T(8,128)(2,1)}, u32[]{:S(2)}, u32[]{:S(2)}) collective-permute-start(bf16[160,896]{1,0:T(8,128)(2,1)} %fusion.17), channel_id=1, source_target_pairs={{0,56},{8,0},{16,8},{24,16},{32,24},{40,32},{48,40},{56,48},{1,57}... | collective-permute-start | bytes 860168 | tf_op jit(solution)/shard_map/ppermute | solution.py:13
  235.9 2.2 fusion.1
  238.1 3.7 %stack_reshape.7 = f32[1,2,2,320,320]{3,2,1,4,0:T(2,128)} reshape(f32[1280,320]{0,1:T(8,128)} %fusion.1) | data formatting | bytes 3276800 | tf_op jit(solution)/shard_map/stack;reshape | solution.py:107
  241.8 5.1 %copy.16 = f32[1,2,2,320,320]{4,3,1,0,2:T(8,128)} copy(f32[1,2,2,320,320]{3,2,1,4,0:T(2,128)} %stack_reshape.7) | data formatting | bytes 3276800 | tf_op jit(solution)/shard_map/stack;reshape | solution.py:107
  246.9 1.4 fusion.20
  248.5 1.4 add_convert_fusion.4
  250.0 1.4 add_convert_fusion.2
  251.4 3.2 %collective-permute-start.23 = (bf16[160,896]{1,0:T(8,128)(2,1)S(1)}, bf16[160,896]{1,0:T(8,128)(2,1)S(1)}, u32[]{:S(2)}, u32[]{:S(2)}) collective-permute-start(bf16[160,896]{1,0:T(8,128)(2,1)S(1)} %add_convert_fusion.2), channel_id=1, source_target_pairs={{0,56},{8,0},{16,8},{24,16},{32,24},{40,32},{48,40},{56,48},{1,57}... | collective-permute-start | bytes 860168 | tf_op jit(solution)/shard_map/ppermute | solution.py:13
  254.6 1.3 add_convert_fusion.9
  256.0 1.3 add_convert_fusion.6
  257.4 3.2 %collective-permute-start.17 = (bf16[160,896]{1,0:T(8,128)(2,1)S(1)}, bf16[160,896]{1,0:T(8,128)(2,1)S(1)}, u32[]{:S(2)}, u32[]{:S(2)}) collective-permute-start(bf16[160,896]{1,0:T(8,128)(2,1)S(1)} %add_convert_fusion.6), channel_id=1, source_target_pairs={{0,56},{8,0},{16,8},{24,16},{32,24},{40,32},{48,40},{56,48},{1,57}... | collective-permute-start | bytes 860168 | tf_op jit(solution)/shard_map/ppermute | solution.py:13
  261.9 3.8 %collective-permute-start.24 = (bf16[160,896]{1,0:T(8,128)(2,1)S(1)}, bf16[160,896]{1,0:T(8,128)(2,1)S(1)}, u32[]{:S(2)}, u32[]{:S(2)}) collective-permute-start(bf16[160,896]{1,0:T(8,128)(2,1)S(1)} %add_convert_fusion.1), channel_id=1, source_target_pairs={{0,56},{8,0},{16,8},{24,16},{32,24},{40,32},{48,40},{56,48},{1,57}... | collective-permute-start | bytes 860168 | tf_op jit(solution)/shard_map/ppermute | solution.py:13
  265.7 1.2 collective-permute-done.13
  268.2 3.8 %collective-permute-start.18 = (bf16[160,896]{1,0:T(8,128)(2,1)S(1)}, bf16[160,896]{1,0:T(8,128)(2,1)S(1)}, u32[]{:S(2)}, u32[]{:S(2)}) collective-permute-start(bf16[160,896]{1,0:T(8,128)(2,1)S(1)} %add_convert_fusion.5), channel_id=1, source_target_pairs={{0,56},{8,0},{16,8},{24,16},{32,24},{40,32},{48,40},{56,48},{1,57}... | collective-permute-start | bytes 860168 | tf_op jit(solution)/shard_map/ppermute | solution.py:13
  274.0 1.2 collective-permute-start.4
  275.5 3.2 %collective-permute-done.14 = bf16[160,896]{1,0:T(8,128)(2,1)S(1)} collective-permute-done((bf16[160,896]{1,0:T(8,128)(2,1)S(1)}, bf16[160,896]{1,0:T(8,128)(2,1)S(1)}, u32[]{:S(2)}, u32[]{:S(2)}) %collective-permute-start.14) | collective-permute-done | bytes 286752 | tf_op jit(solution)/shard_map/ppermute | solution.py:13
  279.7 3.2 %collective-permute-done.3 = bf16[320,320]{1,0:T(8,128)(2,1)S(1)} collective-permute-done((bf16[320,320]{1,0:T(8,128)(2,1)S(1)}, bf16[320,320]{1,0:T(8,128)(2,1)S(1)}, u32[]{:S(2)}, u32[]{:S(2)}) %collective-permute-start.3) | collective-permute-done | bytes 204832 | tf_op jit(solution)/shard_map/ppermute | solution.py:20
  282.9 2.5 collective-permute-done.4
  286.7 2.8 collective-permute-done.25
  289.9 5.6 %collective-permute-done.15 = bf16[160,896]{1,0:T(8,128)(2,1)S(1)} collective-permute-done((bf16[160,896]{1,0:T(8,128)(2,1)S(1)}, bf16[160,896]{1,0:T(8,128)(2,1)S(1)}, u32[]{:S(2)}, u32[]{:S(2)}) %collective-permute-start.15) | collective-permute-done | bytes 286752 | tf_op jit(solution)/shard_map/ppermute | solution.py:13
  296.1 2.6 collective-permute-start.27
  298.8 1.7 collective-permute-start.28
  300.5 1.2 fusion.15
  301.6 3.4 %collective-permute-done.26 = bf16[40,1792]{1,0:T(8,128)(2,1)S(1)} collective-permute-done((bf16[40,1792]{1,0:T(8,128)(2,1)S(1)}, bf16[40,1792]{1,0:T(8,128)(2,1)S(1)}, u32[]{:S(2)}, u32[]{:S(2)}) %collective-permute-start.26) | collective-permute-done | bytes 143392 | tf_op jit(solution)/shard_map/ppermute | solution.py:13
  (148 shorter events, 24.1 us)
Async XLA Ops:
  7.2 2.5 copy-start
  7.2 85.1 %all-gather.3.cloned.1.call-start = ((), (), s32[]{:S(2)}) async-start(), calls=%async_computation | async-start | bytes 2365440 | tf_op jit(solution)/shard_map/all_gather | solution.py:47
  8.9 161.7 %all-gather.5.cloned.1.call-start = ((), (), s32[]{:S(2)}) async-start(), calls=%async_computation.1 | async-start | bytes 2365440 | tf_op jit(solution)/shard_map/all_gather | solution.py:47
  11.7 8.9 %collective-permute-start.7 = (bf16[320,320]{1,0:T(8,128)(2,1)S(1)}, bf16[320,320]{1,0:T(8,128)(2,1)S(1)}, u32[]{:S(2)}, u32[]{:S(2)}) collective-permute-start(bf16[320,320]{1,0:T(8,128)(2,1)S(1)} %get-tuple-element.41), channel_id=1, source_target_pairs={{0,6},{4,0},{2,4},{6,2},{1,7},{5,1},{3,5},{7,3},{8,14},{12,8},{10,... | collective-permute-start | bytes 614408 | tf_op jit(solution)/shard_map/ppermute | solution.py:20
  12.3 8.6 %collective-permute-start.8 = (bf16[320,320]{1,0:T(8,128)(2,1)S(1)}, bf16[320,320]{1,0:T(8,128)(2,1)S(1)}, u32[]{:S(2)}, u32[]{:S(2)}) collective-permute-start(bf16[320,320]{1,0:T(8,128)(2,1)S(1)} %get-tuple-element.41), channel_id=1, source_target_pairs={{0,4},{4,2},{2,6},{6,0},{1,5},{5,3},{3,7},{7,1},{8,12},{12,10},{10... | collective-permute-start | bytes 614408 | tf_op jit(solution)/shard_map/ppermute | solution.py:20
  13.8 12.2 %collective-permute-start.6 = (bf16[320,320]{1,0:T(8,128)(2,1)S(1)}, bf16[320,320]{1,0:T(8,128)(2,1)S(1)}, u32[]{:S(2)}, u32[]{:S(2)}) collective-permute-start(bf16[320,320]{1,0:T(8,128)(2,1)S(1)} %bitcast.197), channel_id=1, source_target_pairs={{0,2},{4,6},{2,0},{6,4},{1,3},{5,7},{3,1},{7,5},{8,10},{12,14},{10... | collective-permute-start | bytes 614408 | tf_op jit(solution)/shard_map/ppermute | solution.py:20
  26.0 3.0 copy-start.28
  26.2 2.7 collective-permute-start.9
  30.4 140.2 %copy-start.31 = (bf16[320,320]{1,0:T(8,128)(2,1)S(1)}, bf16[320,320]{1,0:T(8,128)(2,1)}, u32[]{:S(2)}) copy-start(bf16[320,320]{1,0:T(8,128)(2,1)} %copy-done.30) | copy-start | bytes 614404
  30.4 140.2 %copy-start.33 = (bf16[320,320]{1,0:T(8,128)(2,1)S(1)}, bf16[320,320]{1,0:T(8,128)(2,1)}, u32[]{:S(2)}) copy-start(bf16[320,320]{1,0:T(8,128)(2,1)} %copy-done.32) | copy-start | bytes 614404
  30.4 140.2 %copy-start.35 = (bf16[320,320]{1,0:T(8,128)(2,1)S(1)}, bf16[320,320]{1,0:T(8,128)(2,1)}, u32[]{:S(2)}) copy-start(bf16[320,320]{1,0:T(8,128)(2,1)} %copy-done.34) | copy-start | bytes 614404
  30.5 140.2 %copy-start.37 = (bf16[320,320]{1,0:T(8,128)(2,1)S(1)}, bf16[320,320]{1,0:T(8,128)(2,1)}, u32[]{:S(2)}) copy-start(bf16[320,320]{1,0:T(8,128)(2,1)} %copy-done.36) | copy-start | bytes 614404
  96.2 79.7 %collective-permute-start.10 = (bf16[320,896]{1,0:T(8,128)(2,1)}, bf16[320,896]{1,0:T(8,128)(2,1)}, u32[]{:S(2)}, u32[]{:S(2)}) collective-permute-start(bf16[320,896]{1,0:T(8,128)(2,1)} %convolution_convert_fusion.1), channel_id=1, source_target_pairs={{0,4},{4,0},{1,5},{5,1},{2,6},{6,2},{3,7},{7,3},{8,12},{12,8},{9,1... | collective-permute-start | bytes 1720328 | tf_op jit(solution)/shard_map/ppermute | solution.py:13
  173.3 11.0 %collective-permute-start.11 = (bf16[320,896]{1,0:T(8,128)(2,1)S(1)}, bf16[320,896]{1,0:T(8,128)(2,1)S(1)}, u32[]{:S(2)}, u32[]{:S(2)}) collective-permute-start(bf16[320,896]{1,0:T(8,128)(2,1)S(1)} %convolution_convert_fusion), channel_id=1, source_target_pairs={{0,4},{4,0},{1,5},{5,1},{2,6},{6,2},{3,7},{7,3},{8,12},{12,8},{9,1... | collective-permute-start | bytes 1720328 | tf_op jit(solution)/shard_map/ppermute | solution.py:13
  175.9 8.3 %copy-start.5 = (bf16[1280,896]{1,0:T(8,128)(2,1)S(1)}, bf16[1280,896]{1,0:T(8,128)(2,1)}, u32[]{:S(2)}) copy-start(bf16[1280,896]{1,0:T(8,128)(2,1)} %all-gather.5.cloned.1.call-done) | copy-start | bytes 6881284
  178.9 6.5 %copy-start.21 = (bf16[320,1792]{1,0:T(8,128)(2,1)S(1)}, bf16[320,1792]{1,0:T(8,128)(2,1)}, u32[]{:S(2)}) copy-start(bf16[320,1792]{1,0:T(8,128)(2,1)} %param.5) | copy-start | bytes 3440644
  178.9 6.5 %copy-start.22 = (bf16[320,1792]{1,0:T(8,128)(2,1)S(1)}, bf16[320,1792]{1,0:T(8,128)(2,1)}, u32[]{:S(2)}) copy-start(bf16[320,1792]{1,0:T(8,128)(2,1)} %param.6) | copy-start | bytes 3440644
  205.3 16.1 %collective-permute-start.1 = (bf16[320,896]{1,0:T(8,128)(2,1)}, bf16[320,896]{1,0:T(8,128)(2,1)S(1)}, u32[]{:S(2)}, u32[]{:S(2)}) collective-permute-start(bf16[320,896]{1,0:T(8,128)(2,1)} %get-tuple-element.21), channel_id=1, source_target_pairs={{0,4},{4,0},{1,5},{5,1},{2,6},{6,2},{3,7},{7,3},{8,12},{12,8},{9,1... | collective-permute-start | bytes 1720328 | tf_op jit(solution)/shard_map/ppermute | solution.py:13
  206.5 22.9 %collective-permute-start = (bf16[320,896]{1,0:T(8,128)(2,1)}, bf16[320,896]{1,0:T(8,128)(2,1)S(1)}, u32[]{:S(2)}, u32[]{:S(2)}) collective-permute-start(bf16[320,896]{1,0:T(8,128)(2,1)} %get-tuple-element.20), channel_id=1, source_target_pairs={{0,4},{4,0},{1,5},{5,1},{2,6},{6,2},{3,7},{7,3},{8,12},{12,8},{9,1... | collective-permute-start | bytes 1720328 | tf_op jit(solution)/shard_map/ppermute | solution.py:13
  218.5 11.0 %copy-start.20 = (f32[160,896]{1,0:T(8,128)S(1)}, f32[160,896]{1,0:T(8,128)}, u32[]{:S(2)}) copy-start(f32[160,896]{1,0:T(8,128)} %fusion.73) | copy-start | bytes 1720324
  218.5 11.0 %copy-start.38 = (bf16[4,1,40,320]{3,2,1,0:T(8,128)(2,1)S(1)}, bf16[4,1,40,320]{3,2,1,0:T(8,128)(2,1)}, u32[]{:S(2)}) copy-start(bf16[4,1,40,320]{3,2,1,0:T(8,128)(2,1)} %get-tuple-element.30) | copy-start | bytes 307204
  221.5 9.0 %copy-start.19 = (f32[160,896]{1,0:T(8,128)S(1)}, f32[160,896]{1,0:T(8,128)}, u32[]{:S(2)}) copy-start(f32[160,896]{1,0:T(8,128)} %fusion.65) | copy-start | bytes 1720324
  221.5 9.0 %copy-start.25 = (bf16[4,1,40,320]{3,2,1,0:T(8,128)(2,1)S(1)}, bf16[4,1,40,320]{3,2,1,0:T(8,128)(2,1)}, u32[]{:S(2)}) copy-start(bf16[4,1,40,320]{3,2,1,0:T(8,128)(2,1)} %get-tuple-element.26) | copy-start | bytes 307204
  223.7 24.8 %collective-permute-start.19 = (bf16[160,896]{1,0:T(8,128)(2,1)}, bf16[160,896]{1,0:T(8,128)(2,1)}, u32[]{:S(2)}, u32[]{:S(2)}) collective-permute-start(bf16[160,896]{1,0:T(8,128)(2,1)} %fusion.18), channel_id=1, source_target_pairs={{0,8},{8,16},{16,24},{24,32},{32,40},{40,48},{48,56},{56,0},{1,9},... | collective-permute-start | bytes 860168 | tf_op jit(solution)/shard_map/ppermute | solution.py:13
  224.8 10.0 %copy-start.6 = (bf16[1280,896]{1,0:T(8,128)(2,1)S(1)}, bf16[1280,896]{1,0:T(8,128)(2,1)}, u32[]{:S(2)}) copy-start(bf16[1280,896]{1,0:T(8,128)(2,1)} %all-gather.5.cloned.1.call-done) | copy-start | bytes 6881284
  227.1 22.9 %collective-permute-start.22 = (bf16[160,896]{1,0:T(8,128)(2,1)}, bf16[160,896]{1,0:T(8,128)(2,1)}, u32[]{:S(2)}, u32[]{:S(2)}) collective-permute-start(bf16[160,896]{1,0:T(8,128)(2,1)} %fusion.19), channel_id=1, source_target_pairs={{0,56},{8,0},{16,8},{24,16},{32,24},{40,32},{48,40},{56,48},{1,57}... | collective-permute-start | bytes 860168 | tf_op jit(solution)/shard_map/ppermute | solution.py:13
  230.5 24.1 %collective-permute-start.12 = (bf16[160,896]{1,0:T(8,128)(2,1)}, bf16[160,896]{1,0:T(8,128)(2,1)}, u32[]{:S(2)}, u32[]{:S(2)}) collective-permute-start(bf16[160,896]{1,0:T(8,128)(2,1)} %fusion.16), channel_id=1, source_target_pairs={{0,8},{8,16},{16,24},{24,32},{32,40},{40,48},{48,56},{56,0},{1,9},... | collective-permute-start | bytes 860168 | tf_op jit(solution)/shard_map/ppermute | solution.py:13
  231.5 4.3 %copy-start.4 = (bf16[1280,896]{1,0:T(8,128)(2,1)S(1)}, bf16[1280,896]{1,0:T(8,128)(2,1)}, u32[]{:S(2)}) copy-start(bf16[1280,896]{1,0:T(8,128)(2,1)} %all-gather.3.cloned.1.call-done) | copy-start | bytes 6881284
  231.6 24.4 %collective-permute-start.16 = (bf16[160,896]{1,0:T(8,128)(2,1)}, bf16[160,896]{1,0:T(8,128)(2,1)}, u32[]{:S(2)}, u32[]{:S(2)}) collective-permute-start(bf16[160,896]{1,0:T(8,128)(2,1)} %fusion.17), channel_id=1, source_target_pairs={{0,56},{8,0},{16,8},{24,16},{32,24},{40,32},{48,40},{56,48},{1,57}... | collective-permute-start | bytes 860168 | tf_op jit(solution)/shard_map/ppermute | solution.py:13
  246.9 3.1 copy-start.26
  248.3 6.2 %copy-start.16 = (f32[160,896]{1,0:T(8,128)S(1)}, f32[160,896]{1,0:T(8,128)}, u32[]{:S(2)}) copy-start(f32[160,896]{1,0:T(8,128)} %fusion.71) | copy-start | bytes 1720324
  248.3 6.2 %copy-start.24 = (bf16[4,1,40,320]{3,2,1,0:T(8,128)(2,1)S(1)}, bf16[4,1,40,320]{3,2,1,0:T(8,128)(2,1)}, u32[]{:S(2)}) copy-start(bf16[4,1,40,320]{3,2,1,0:T(8,128)(2,1)} %get-tuple-element.29) | copy-start | bytes 307204
  248.4 23.6 %collective-permute-start.2 = (bf16[2,2,320,320]{3,2,1,0:T(8,128)(2,1)S(1)}, bf16[2,2,320,320]{3,2,1,0:T(8,128)(2,1)S(1)}, u32[]{:S(2)}, u32[]{:S(2)}) collective-permute-start(bf16[2,2,320,320]{3,2,1,0:T(8,128)(2,1)S(1)} %fusion.20), channel_id=1, source_target_pairs={{0,1},{1,0},{2,3},{3,2},{4,5},{5,4},{6,7},{7,6},{8,9},{9,8},{10,11... | collective-permute-start | bytes 2457608 | tf_op jit(solution)/shard_map/ppermute | solution.py:13
  249.8 6.2 %copy-start.15 = (f32[160,896]{1,0:T(8,128)S(1)}, f32[160,896]{1,0:T(8,128)}, u32[]{:S(2)}) copy-start(f32[160,896]{1,0:T(8,128)} %fusion.63) | copy-start | bytes 1720324
  249.9 6.2 %copy-start.23 = (bf16[4,1,40,320]{3,2,1,0:T(8,128)(2,1)S(1)}, bf16[4,1,40,320]{3,2,1,0:T(8,128)(2,1)}, u32[]{:S(2)}) copy-start(bf16[4,1,40,320]{3,2,1,0:T(8,128)(2,1)} %get-tuple-element.25) | copy-start | bytes 307204
  249.9 10.9 %collective-permute-start.20 = (bf16[160,896]{1,0:T(8,128)(2,1)S(1)}, bf16[160,896]{1,0:T(8,128)(2,1)S(1)}, u32[]{:S(2)}, u32[]{:S(2)}) collective-permute-start(bf16[160,896]{1,0:T(8,128)(2,1)S(1)} %add_convert_fusion.4), channel_id=1, source_target_pairs={{0,8},{8,16},{16,24},{24,32},{32,40},{40,48},{48,56},{56,0},{1,9},... | collective-permute-start | bytes 860168 | tf_op jit(solution)/shard_map/ppermute | solution.py:13
  251.4 9.4 %copy-start.13 = (f32[160,896]{1,0:T(8,128)S(1)}, f32[160,896]{1,0:T(8,128)}, u32[]{:S(2)}) copy-start(f32[160,896]{1,0:T(8,128)} %fusion.52) | copy-start | bytes 1720324
  251.4 10.2 %collective-permute-start.23 = (bf16[160,896]{1,0:T(8,128)(2,1)S(1)}, bf16[160,896]{1,0:T(8,128)(2,1)S(1)}, u32[]{:S(2)}, u32[]{:S(2)}) collective-permute-start(bf16[160,896]{1,0:T(8,128)(2,1)S(1)} %add_convert_fusion.2), channel_id=1, source_target_pairs={{0,56},{8,0},{16,8},{24,16},{32,24},{40,32},{48,40},{56,48},{1,57}... | collective-permute-start | bytes 860168 | tf_op jit(solution)/shard_map/ppermute | solution.py:13
  255.9 5.7 %copy-start.14 = (f32[160,896]{1,0:T(8,128)S(1)}, f32[160,896]{1,0:T(8,128)}, u32[]{:S(2)}) copy-start(f32[160,896]{1,0:T(8,128)} %fusion.46) | copy-start | bytes 1720324
  255.9 11.0 %collective-permute-start.13 = (bf16[160,896]{1,0:T(8,128)(2,1)S(1)}, bf16[160,896]{1,0:T(8,128)(2,1)S(1)}, u32[]{:S(2)}, u32[]{:S(2)}) collective-permute-start(bf16[160,896]{1,0:T(8,128)(2,1)S(1)} %add_convert_fusion.9), channel_id=1, source_target_pairs={{0,8},{8,16},{16,24},{24,32},{32,40},{40,48},{48,56},{56,0},{1,9},... | collective-permute-start | bytes 860168 | tf_op jit(solution)/shard_map/ppermute | solution.py:13
  257.4 9.6 %copy-start.12 = (f32[160,896]{1,0:T(8,128)S(1)}, f32[160,896]{1,0:T(8,128)}, u32[]{:S(2)}) copy-start(f32[160,896]{1,0:T(8,128)} %fusion.69) | copy-start | bytes 1720324
  257.4 10.5 %collective-permute-start.17 = (bf16[160,896]{1,0:T(8,128)(2,1)S(1)}, bf16[160,896]{1,0:T(8,128)(2,1)S(1)}, u32[]{:S(2)}, u32[]{:S(2)}) collective-permute-start(bf16[160,896]{1,0:T(8,128)(2,1)S(1)} %add_convert_fusion.6), channel_id=1, source_target_pairs={{0,56},{8,0},{16,8},{24,16},{32,24},{40,32},{48,40},{56,48},{1,57}... | collective-permute-start | bytes 860168 | tf_op jit(solution)/shard_map/ppermute | solution.py:13
  261.1 6.7 %copy-start.11 = (f32[160,896]{1,0:T(8,128)S(1)}, f32[160,896]{1,0:T(8,128)}, u32[]{:S(2)}) copy-start(f32[160,896]{1,0:T(8,128)} %fusion.61) | copy-start | bytes 1720324
  261.1 25.6 %collective-permute-start.21 = (bf16[160,896]{1,0:T(8,128)(2,1)S(1)}, bf16[160,896]{1,0:T(8,128)(2,1)S(1)}, u32[]{:S(2)}, u32[]{:S(2)}) collective-permute-start(bf16[160,896]{1,0:T(8,128)(2,1)S(1)} %add_convert_fusion.3), channel_id=1, source_target_pairs={{0,8},{8,16},{16,24},{24,32},{32,40},{40,48},{48,56},{56,0},{1,9},... | collective-permute-start | bytes 860168 | tf_op jit(solution)/shard_map/ppermute | solution.py:13
  261.9 10.1 %copy-start.2 = (f32[1,2,2,320,320]{4,3,1,0,2:T(8,128)S(1)}, f32[1,2,2,320,320]{4,3,1,0,2:T(8,128)}, u32[]{:S(2)}) copy-start(f32[1,2,2,320,320]{4,3,1,0,2:T(8,128)} %copy.16) | copy-start | bytes 4915204
  261.9 12.1 %collective-permute-start.24 = (bf16[160,896]{1,0:T(8,128)(2,1)S(1)}, bf16[160,896]{1,0:T(8,128)(2,1)S(1)}, u32[]{:S(2)}, u32[]{:S(2)}) collective-permute-start(bf16[160,896]{1,0:T(8,128)(2,1)S(1)} %add_convert_fusion.1), channel_id=1, source_target_pairs={{0,56},{8,0},{16,8},{24,16},{32,24},{40,32},{48,40},{56,48},{1,57}... | collective-permute-start | bytes 860168 | tf_op jit(solution)/shard_map/ppermute | solution.py:13
  267.3 11.5 %collective-permute-start.14 = (bf16[160,896]{1,0:T(8,128)(2,1)S(1)}, bf16[160,896]{1,0:T(8,128)(2,1)S(1)}, u32[]{:S(2)}, u32[]{:S(2)}) collective-permute-start(bf16[160,896]{1,0:T(8,128)(2,1)S(1)} %add_convert_fusion.8), channel_id=1, source_target_pairs={{0,8},{8,16},{16,24},{24,32},{32,40},{40,48},{48,56},{56,0},{1,9},... | collective-permute-start | bytes 860168 | tf_op jit(solution)/shard_map/ppermute | solution.py:13
  268.2 21.6 %collective-permute-start.18 = (bf16[160,896]{1,0:T(8,128)(2,1)S(1)}, bf16[160,896]{1,0:T(8,128)(2,1)S(1)}, u32[]{:S(2)}, u32[]{:S(2)}) collective-permute-start(bf16[160,896]{1,0:T(8,128)(2,1)S(1)} %add_convert_fusion.5), channel_id=1, source_target_pairs={{0,56},{8,0},{16,8},{24,16},{32,24},{40,32},{48,40},{56,48},{1,57}... | collective-permute-start | bytes 860168 | tf_op jit(solution)/shard_map/ppermute | solution.py:13
  272.2 3.0 copy-start.10
  272.2 7.1 %copy-start.9 = (f32[160,896]{1,0:T(8,128)S(1)}, f32[160,896]{1,0:T(8,128)}, u32[]{:S(2)}) copy-start(f32[160,896]{1,0:T(8,128)} %fusion.67) | copy-start | bytes 1720324
  272.4 10.5 %collective-permute-start.3 = (bf16[320,320]{1,0:T(8,128)(2,1)S(1)}, bf16[320,320]{1,0:T(8,128)(2,1)S(1)}, u32[]{:S(2)}, u32[]{:S(2)}) collective-permute-start(bf16[320,320]{1,0:T(8,128)(2,1)S(1)} %get-tuple-element.44), channel_id=1, source_target_pairs={{0,2},{4,6},{2,0},{6,4},{1,3},{5,7},{3,1},{7,5},{8,10},{12,14},{10... | collective-permute-start | bytes 614408 | tf_op jit(solution)/shard_map/ppermute | solution.py:20
  274.0 12.2 %copy-start.39 = (bf16[320,640]{1,0:T(8,128)(2,1)S(1)}, bf16[320,640]{1,0:T(8,128)(2,1)}, u32[]{:S(2)}) copy-start(bf16[320,640]{1,0:T(8,128)(2,1)} %constant.246) | copy-start | bytes 1228804
  274.0 11.4 %collective-permute-start.4 = (bf16[320,320]{1,0:T(8,128)(2,1)S(1)}, bf16[320,320]{1,0:T(8,128)(2,1)S(1)}, u32[]{:S(2)}, u32[]{:S(2)}) collective-permute-start(bf16[320,320]{1,0:T(8,128)(2,1)S(1)} %get-tuple-element.6), channel_id=1, source_target_pairs={{0,4},{4,2},{2,6},{6,0},{1,5},{5,3},{3,7},{7,1},{8,12},{12,10},{10... | collective-permute-start | bytes 614408 | tf_op jit(solution)/shard_map/ppermute | solution.py:20
  278.8 10.7 %copy-start.8 = (f32[160,896]{1,0:T(8,128)S(1)}, f32[160,896]{1,0:T(8,128)}, u32[]{:S(2)}) copy-start(f32[160,896]{1,0:T(8,128)} %fusion.42) | copy-start | bytes 1720324
  278.8 10.7 %copy-start.27 = (bf16[4,1,40,320]{3,2,1,0:T(8,128)(2,1)S(1)}, bf16[4,1,40,320]{3,2,1,0:T(8,128)(2,1)}, u32[]{:S(2)}) copy-start(bf16[4,1,40,320]{3,2,1,0:T(8,128)(2,1)} %get-tuple-element.23) | copy-start | bytes 307204
  278.8 7.5 %collective-permute-start.5 = (bf16[320,320]{1,0:T(8,128)(2,1)S(1)}, bf16[320,320]{1,0:T(8,128)(2,1)S(1)}, u32[]{:S(2)}, u32[]{:S(2)}) collective-permute-start(bf16[320,320]{1,0:T(8,128)(2,1)S(1)} %get-tuple-element.7), channel_id=1, source_target_pairs={{0,6},{4,0},{2,4},{6,2},{1,7},{5,1},{3,5},{7,3},{8,14},{12,8},{10,... | collective-permute-start | bytes 614408 | tf_op jit(solution)/shard_map/ppermute | solution.py:20
  282.9 6.6 %collective-permute-start.25 = (bf16[160,896]{1,0:T(8,128)(2,1)S(1)}, bf16[160,896]{1,0:T(8,128)(2,1)S(1)}, u32[]{:S(2)}, u32[]{:S(2)}) collective-permute-start(bf16[160,896]{1,0:T(8,128)(2,1)S(1)} %add_convert_fusion), channel_id=1, source_target_pairs={{0,56},{8,0},{16,8},{24,16},{32,24},{40,32},{48,40},{56,48},{1,57}... | collective-permute-start | bytes 860168 | tf_op jit(solution)/shard_map/ppermute | solution.py:13
  282.9 12.5 %copy-start.7 = (f32[160,896]{1,0:T(8,128)S(1)}, f32[160,896]{1,0:T(8,128)}, u32[]{:S(2)}) copy-start(f32[160,896]{1,0:T(8,128)} %fusion.59) | copy-start | bytes 1720324
  285.4 10.0 %collective-permute-start.15 = (bf16[160,896]{1,0:T(8,128)(2,1)S(1)}, bf16[160,896]{1,0:T(8,128)(2,1)S(1)}, u32[]{:S(2)}, u32[]{:S(2)}) collective-permute-start(bf16[160,896]{1,0:T(8,128)(2,1)S(1)} %add_convert_fusion.7), channel_id=1, source_target_pairs={{0,8},{8,16},{16,24},{24,32},{32,40},{40,48},{48,56},{56,0},{1,9},... | collective-permute-start | bytes 860168 | tf_op jit(solution)/shard_map/ppermute | solution.py:13
  289.8 10.6 %copy-start.40 = (bf16[320,640]{1,0:T(8,128)(2,1)S(1)}, bf16[320,640]{1,0:T(8,128)(2,1)}, u32[]{:S(2)}) copy-start(bf16[320,640]{1,0:T(8,128)(2,1)} %constant.245) | copy-start | bytes 1228804
  295.8 9.2 %collective-permute-start.26 = (bf16[40,1792]{1,0:T(8,128)(2,1)S(1)}, bf16[40,1792]{1,0:T(8,128)(2,1)S(1)}, u32[]{:S(2)}, u32[]{:S(2)}) collective-permute-start(bf16[40,1792]{1,0:T(8,128)(2,1)S(1)} %get-tuple-element.17), channel_id=1, source_target_pairs={{0,64},{64,128},{128,192},{192,0},{1,65},{65,129},{129,193},{193,1... | collective-permute-start | bytes 430088 | tf_op jit(solution)/shard_map/ppermute | solution.py:13
  296.1 8.9 %collective-permute-start.27 = (bf16[40,1792]{1,0:T(8,128)(2,1)S(1)}, bf16[40,1792]{1,0:T(8,128)(2,1)S(1)}, u32[]{:S(2)}, u32[]{:S(2)}) collective-permute-start(bf16[40,1792]{1,0:T(8,128)(2,1)S(1)} %get-tuple-element.18), channel_id=1, source_target_pairs={{0,128},{64,192},{128,0},{192,64},{1,129},{65,193},{129,1},{193,65... | collective-permute-start | bytes 430088 | tf_op jit(solution)/shard_map/ppermute | solution.py:13
  298.8 7.6 %copy-start.1 = (bf16[320,640]{1,0:T(8,128)(2,1)S(1)}, bf16[320,640]{1,0:T(8,128)(2,1)}, u32[]{:S(2)}) copy-start(bf16[320,640]{1,0:T(8,128)(2,1)} %param.8) | copy-start | bytes 1228804
  298.8 6.8 %collective-permute-start.28 = (bf16[40,1792]{1,0:T(8,128)(2,1)S(1)}, bf16[40,1792]{1,0:T(8,128)(2,1)S(1)}, u32[]{:S(2)}, u32[]{:S(2)}) collective-permute-start(bf16[40,1792]{1,0:T(8,128)(2,1)S(1)} %get-tuple-element.19), channel_id=1, source_target_pairs={{0,192},{64,0},{128,64},{192,128},{1,193},{65,1},{129,65},{193,129... | collective-permute-start | bytes 430088 | tf_op jit(solution)/shard_map/ppermute | solution.py:13
  (8 other events, 9.6 us)
Sparse Core Ops, SparseCore 0:
  10.6 81.5 all-gather.2
  94.8 75.7 all-gather.4
